TPU v7x, 32 devices: a whole 2x2x4 slice. The times are simulated.
32 devices in a mesh: rep: 2 (over x), cand: 16 (over z, y, core).
Axes of the slice: x: 2, y: 2, z: 4, core: 2. Of those that a mesh axis runs over, the one named last changes fastest.
Arguments:
- layer_activations: bfloat16 [64, 2, 8192], P(('rep', 'cand')), parts along dimension 0, may hold values from -6 to 6
- entry_scaling_factor: bfloat16 [8192], replicated, may hold values from 0.5 to 2
- asker_matrix: bfloat16 [8192, 8192], P(None, 'cand'), may hold values from -0.0625 to 0.0625
- address_matrix: bfloat16 [8192, 1024], P(None, 'cand'), may hold values from -0.0625 to 0.0625
- content_matrix: bfloat16 [8192, 1024], P(None, 'cand'), may hold values from -0.0625 to 0.0625
- final_matrix: bfloat16 [8192, 8192], P('cand'), may hold values from -0.1875 to 0.1875
- candidate_memory_blocks: bfloat16 [4096, 8, 2048], P(('rep', 'cand')), parts along dimension 0, may hold values from -64 to 64
- winning_candidates: int32 [64], P('rep'), parts along dimension 0, may hold values from 0 to 63, as said below
- winner_chip_assignment: int32 [64], P('rep'), parts along dimension 0, may hold values from 0 to 15, as said below
- candidate_block_map: int32 [128, 32], P('rep'), parts along dimension 0, may hold values from 0 to 2047, as said below
- candidate_filled_extent: int32 [128], P('rep'), parts along dimension 0, may hold values from 1 to 256
Outputs:
- mixing_result: bfloat16 [64, 2, 8192], P(('rep', 'cand')), parts along dimension 0
- winner_memory_blocks: bfloat16 [64, 32, 8, 2048], P(('rep', 'cand')), parts along dimension 0
There are 2 independent parts, one for each index of `rep`. A program takes and returns all parts, laid end to end along the dimension named above; an argument that names none is the same for every part. Nothing has to cross between parts.
Inputs may be any that keep to these rules, and one draw needn't show every extreme that they name: `winning_candidates`: 32 distinct ids. `winner_chip_assignment`: every device index appears exactly 2 times. `candidate_block_map`: every page id appears exactly once in the table; for every device s, the pages that s holds of survivors placed on device d number 4 for all d but two: for one d they number 2 * 4, for another none.
All inputs are finite; a program needn't handle non-finite values.
Results may differ from a plain program's by a relative error of at most 0.006.
The roundings to bfloat16 on the way count: a program that leaves them out, or rounds other values in their place, can miss the bound.
Values may be sent and summed in bfloat16 or wider, within the bound.
A program may use at most 128 MiB of HBM per device.

v0:
```python
import math

import jax
import jax.numpy as jnp
from jax import lax
from jax.sharding import PartitionSpec as P

ASKER_UNITS = 64
KV_ATTN_UNITS = 8
ATTN_DIM = 128


EPS = 1e-06
ROPE_BASE = 1000000.0
NEG_FILL = -1e30


def spot_numbering(winner_chip_assignment, per_device):
    position_vector = jnp.arange(winner_chip_assignment.shape[0], dtype=jnp.int32)
    earlier = position_vector[None, :] < position_vector[:, None]
    same_dev = winner_chip_assignment[None, :] == winner_chip_assignment[:, None]
    position_on_chip = jnp.sum(jnp.where(earlier & same_dev, 1, 0), axis=1).astype(jnp.int32)
    return winner_chip_assignment * per_device + position_on_chip


def normalize(row_block, entry_scaling_factor):
    rows_f32 = row_block.astype(jnp.float32)
    mean_sq = jnp.mean(rows_f32 * rows_f32, axis=-1, keepdims=True)
    return (rows_f32 * lax.rsqrt(mean_sq + EPS) * entry_scaling_factor.astype(jnp.float32)).astype(
        jnp.bfloat16
    )


def rotate(vectors, positions):
    half_dim = vectors.shape[-1] // 2
    frequencies = ROPE_BASE ** (
        -(jnp.arange(half_dim, dtype=jnp.float32) * 2.0 / vectors.shape[-1])
    )
    angles = positions.astype(jnp.float32)[..., None] * frequencies
    cosine_table = jnp.cos(angles)[..., None, :]
    sine_table = jnp.sin(angles)[..., None, :]
    first_half = vectors[..., :half_dim]
    second_half = vectors[..., half_dim:]
    return jnp.concatenate(
        [
            first_half * cosine_table - second_half * sine_table,
            second_half * cosine_table + first_half * sine_table,
        ],
        axis=-1,
    )


def relocate_pages(
    candidate_memory_blocks,
    winning_candidates,
    winner_chip_assignment,
    candidate_block_map,
    winner_placement_spot,
    device_index,
    device_count,
    chip_resident_entries,
):
    spots_on_chip = candidate_memory_blocks.shape[0]
    chain_pages = candidate_block_map.shape[1]
    winner_block_map = candidate_block_map[winning_candidates]
    holding_chip = (winner_block_map // spots_on_chip).reshape(-1)
    resident_block = (winner_block_map % spots_on_chip).reshape(-1)
    target_chip = jnp.broadcast_to(winner_chip_assignment[:, None], winner_block_map.shape).reshape(
        -1
    )
    position_on_chip = (winner_placement_spot % chip_resident_entries)[:, None]
    target_pos = (
        position_on_chip * chain_pages + jnp.arange(chain_pages, dtype=jnp.int32)[None, :]
    ).reshape(-1)
    is_mine = holding_chip == device_index
    onehot = jnp.where(
        is_mine[:, None]
        & (target_chip[:, None] == jnp.arange(device_count, dtype=jnp.int32)[None, :]),
        1,
        0,
    )
    order_in = jnp.cumsum(onehot, axis=0) - onehot
    within = jnp.sum(order_in * onehot, axis=1)
    capacity = 2 * (chip_resident_entries * chain_pages // device_count)
    where_to = jnp.where(is_mine, target_chip * capacity + within, device_count * capacity)
    send_page = (
        jnp.zeros((device_count * capacity,), jnp.int32)
        .at[where_to]
        .set(resident_block, mode="drop")
    )
    empty_pos = chip_resident_entries * chain_pages
    send_pos = (
        jnp.full((device_count * capacity,), empty_pos, jnp.int32)
        .at[where_to]
        .set(target_pos, mode="drop")
    )
    outgoing = candidate_memory_blocks[send_page].reshape(
        device_count, capacity, candidate_memory_blocks.shape[1], candidate_memory_blocks.shape[2]
    )
    arrived, positions = (
        lax.all_to_all(outgoing, "cand", split_axis=0, concat_axis=0, tiled=True),
        lax.all_to_all(
            send_pos.reshape(device_count, capacity),
            "cand",
            split_axis=0,
            concat_axis=0,
            tiled=True,
        ),
    )
    gathered = jnp.zeros(
        (empty_pos, candidate_memory_blocks.shape[1], candidate_memory_blocks.shape[2]),
        candidate_memory_blocks.dtype,
    )
    gathered = gathered.at[positions.reshape(-1)].set(
        arrived.reshape(-1, candidate_memory_blocks.shape[1], candidate_memory_blocks.shape[2]),
        mode="drop",
    )
    return gathered.reshape(
        chip_resident_entries,
        chain_pages,
        candidate_memory_blocks.shape[1],
        candidate_memory_blocks.shape[2],
    )


def attend(rotated_query, moved_blocks, context_extents, appended_keys, appended_values, token_ids):
    total_row_count, token_pair_group = (rotated_query.shape[0], rotated_query.shape[1])
    heads_per_device = ASKER_UNITS // KV_ATTN_UNITS
    grouped_queries = rotated_query.reshape(
        total_row_count, token_pair_group, KV_ATTN_UNITS, heads_per_device, ATTN_DIM
    )
    stacked_pages = moved_blocks.reshape(total_row_count, -1, 2, KV_ATTN_UNITS, ATTN_DIM)
    cache_keys = stacked_pages[:, :, 0]
    cache_values = stacked_pages[:, :, 1]
    score_scale = 1.0 / math.sqrt(ATTN_DIM)
    scores_cache = (
        jnp.einsum(
            "btkgd,bskd->btkgs", grouped_queries, cache_keys, preferred_element_type=jnp.float32
        )
        * score_scale
    )
    current_token_keys = appended_keys.reshape(total_row_count, 2, KV_ATTN_UNITS, ATTN_DIM)
    current_token_values = appended_values.reshape(total_row_count, 2, KV_ATTN_UNITS, ATTN_DIM)
    scores_fresh = (
        jnp.einsum(
            "btkgd,bukd->btkgu",
            grouped_queries,
            current_token_keys,
            preferred_element_type=jnp.float32,
        )
        * score_scale
    )
    valid_cache = (
        jnp.arange(stacked_pages.shape[1], dtype=jnp.int32)[None, :] < context_extents[:, None]
    )[:, None, None, None, :]
    valid_fresh = (jnp.arange(2, dtype=jnp.int32)[None, :] <= token_ids[:, None])[
        None, :, None, None, :
    ]
    masked_cache = jnp.where(valid_cache, scores_cache, NEG_FILL)
    masked_fresh = jnp.where(valid_fresh, scores_fresh, NEG_FILL)
    peak_score = jnp.maximum(
        jnp.max(masked_cache, axis=-1, keepdims=True), jnp.max(masked_fresh, axis=-1, keepdims=True)
    )
    exp_cache = jnp.where(valid_cache, jnp.exp(masked_cache - peak_score), 0.0)
    exp_fresh = jnp.where(valid_fresh, jnp.exp(masked_fresh - peak_score), 0.0)
    denominator = jnp.sum(exp_cache, axis=-1, keepdims=True) + jnp.sum(
        exp_fresh, axis=-1, keepdims=True
    )
    weights_cache = (exp_cache / denominator).astype(jnp.bfloat16)
    weights_fresh = (exp_fresh / denominator).astype(jnp.bfloat16)
    combined_channels = jnp.einsum(
        "btkgs,bskd->btkgd", weights_cache, cache_values, preferred_element_type=jnp.float32
    )
    combined_channels = combined_channels + jnp.einsum(
        "btkgu,bukd->btkgd", weights_fresh, current_token_values, preferred_element_type=jnp.float32
    )
    return combined_channels.reshape(
        total_row_count, token_pair_group, ASKER_UNITS * ATTN_DIM
    ).astype(jnp.bfloat16)


def body(
    layer_activations,
    entry_scaling_factor,
    asker_matrix,
    address_matrix,
    content_matrix,
    final_matrix,
    candidate_memory_blocks,
    winning_candidates,
    winner_chip_assignment,
    candidate_block_map,
    candidate_filled_extent,
):
    device_count = lax.axis_size("cand")
    device_index = lax.axis_index("cand")
    chip_resident_entries = layer_activations.shape[0]
    winner_placement_spot = spot_numbering(winner_chip_assignment, chip_resident_entries)
    keep_of_slot = (
        jnp.zeros_like(winner_placement_spot)
        .at[winner_placement_spot]
        .set(jnp.arange(winner_placement_spot.shape[0], dtype=jnp.int32))
    )
    chip_position_array = lax.dynamic_slice_in_dim(
        keep_of_slot, device_index * chip_resident_entries, chip_resident_entries
    )
    context_extents = candidate_filled_extent[winning_candidates[chip_position_array]]
    moved_blocks = relocate_pages(
        candidate_memory_blocks,
        winning_candidates,
        winner_chip_assignment,
        candidate_block_map,
        winner_placement_spot,
        device_index,
        device_count,
        chip_resident_entries,
    )
    joined = jnp.concatenate([asker_matrix, address_matrix, content_matrix], axis=1)
    query_cols = asker_matrix.shape[1]
    key_cols = address_matrix.shape[1]
    source_rows = normalize(layer_activations, entry_scaling_factor)
    token_pair_group = 1
    key_value_width = KV_ATTN_UNITS * ATTN_DIM
    appended_keys = jnp.zeros((chip_resident_entries, 2, key_value_width), jnp.bfloat16)
    appended_values = jnp.zeros((chip_resident_entries, 2, key_value_width), jnp.bfloat16)
    results = []
    for start_token in range(0, 2, token_pair_group):
        token_rows = source_rows[:, start_token : start_token + token_pair_group, :]
        block_rows = lax.all_gather(token_rows, "cand", axis=0, tiled=True)
        product = jnp.dot(
            block_rows.reshape(-1, block_rows.shape[2]), joined, preferred_element_type=jnp.float32
        )
        projected = product.reshape(block_rows.shape[0], block_rows.shape[1], joined.shape[1])
        ordered = projected[keep_of_slot].astype(jnp.bfloat16)
        arrived = lax.all_to_all(ordered, "cand", split_axis=0, concat_axis=2, tiled=True)
        arrived = arrived.reshape(
            chip_resident_entries, token_pair_group, device_count, joined.shape[1]
        )
        asker_vectors = arrived[..., :query_cols].reshape(
            chip_resident_entries, token_pair_group, ASKER_UNITS, ATTN_DIM
        )
        keys_part = arrived[..., query_cols : query_cols + key_cols].reshape(
            chip_resident_entries, token_pair_group, KV_ATTN_UNITS, ATTN_DIM
        )
        values_part = arrived[..., query_cols + key_cols :].reshape(
            chip_resident_entries, token_pair_group, key_value_width
        )
        token_ids = start_token + jnp.arange(token_pair_group, dtype=jnp.int32)
        positions = context_extents[:, None] + token_ids[None, :]
        rotated_query = (
            rotate(asker_vectors.astype(jnp.float32), positions)
            .astype(jnp.bfloat16)
            .reshape(chip_resident_entries, token_pair_group, ASKER_UNITS * ATTN_DIM)
        )
        key_rot = (
            rotate(keys_part.astype(jnp.float32), positions)
            .astype(jnp.bfloat16)
            .reshape(chip_resident_entries, token_pair_group, key_value_width)
        )
        appended_keys = appended_keys.at[:, start_token : start_token + token_pair_group].set(
            key_rot
        )
        appended_values = appended_values.at[:, start_token : start_token + token_pair_group].set(
            values_part
        )
        combined_channels = attend(
            rotated_query, moved_blocks, context_extents, appended_keys, appended_values, token_ids
        )
        heads_here = lax.all_to_all(
            combined_channels, "cand", split_axis=2, concat_axis=0, tiled=True
        )
        out_product = jnp.dot(
            heads_here.reshape(-1, heads_here.shape[2]),
            final_matrix,
            preferred_element_type=jnp.float32,
        )
        results.append(
            lax.psum_scatter(
                out_product.reshape(
                    chip_resident_entries * lax.axis_size("cand"),
                    heads_here.shape[1],
                    final_matrix.shape[1],
                ),
                "cand",
                scatter_dimension=0,
                tiled=True,
            )
        )
    mixing_result = jnp.concatenate(results, axis=1).astype(jnp.bfloat16)
    return (mixing_result, moved_blocks)


def solution(mesh):
    return jax.shard_map(
        body,
        mesh=mesh,
        in_specs=(
            P(("rep", "cand"), None, None),
            P(),
            P(None, "cand"),
            P(None, "cand"),
            P(None, "cand"),
            P("cand", None),
            P(("rep", "cand"), None, None),
            P("rep"),
            P("rep"),
            P("rep", None),
            P("rep"),
        ),
        out_specs=(P(("rep", "cand"), None, None), P(("rep", "cand"), None, None, None)),
        check_vma=False,
    )
```

profile of v0, /device:TPU:0, one launch (start us, length us, event | category | flops | bytes accessed | tf_op | source)
XLA Modules:
  0.0 471.9 jit_solution(11462485366146760597)
XLA Ops:
  0.6 0.9 select_reduce_fusion
  1.6 0.7 broadcast_in_dim.166
  2.3 0.8 copy.147
  3.1 0.7 compare_select_fusion.10
  3.8 0.6 gather_fusion
  4.6 0.7 compare_select_fusion.11
  5.4 4.5 reduce-window.6
  10.4 0.7 broadcast_in_dim.171
  11.6 4.3 scatter_custom_fusion
  15.9 0.7 all_to_all.53
  16.6 7.4 %all-to-all-start = ((s32[16,1,8]{2,1,0:T(1,128)}), s32[16,1,8]{2,1,0:T(1,128)S(1)}, u32[]{:S(2)}, u32[]{:S(2)}) async-start(s32[16,1,8]{2,1,0:T(1,128)} %bitcast.4), calls=%async_computation | async-start | bytes 16384 | tf_op jit(solution)/shard_map/all_to_all | solution.py:102
  24.0 0.7 scatter_custom_fusion.3
  24.7 2.0 copy.153
  26.7 2.7 copy.154
  29.4 0.7 convert_element_type.205
  30.2 1.0 fusion.24
  31.2 1.0 fusion.26
  32.3 24.7 %all_gather.6 = bf16[32,1,8192]{2,1,0:T(2,128)(2,1)S(1)} all-gather(bf16[2,1,8192]{2,1,0:T(2,128)(2,1)S(1)} %get-tuple-element.76), channel_id=1, replica_groups=mesh['rep'=2,'cand'=16] {'cand'}, dimensions={0}, use_global_device_ids=true | all-gather | bytes 557056 | tf_op jit(solution)/shard_map/all_gather | solution.py:229
  57.0 20.8 %all_gather.7 = bf16[32,1,8192]{2,1,0:T(2,128)(2,1)S(1)} all-gather(bf16[2,1,8192]{2,1,0:T(2,128)(2,1)S(1)} %get-tuple-element.77), channel_id=1, replica_groups=mesh['rep'=2,'cand'=16] {'cand'}, dimensions={0}, use_global_device_ids=true | all-gather | bytes 557056 | tf_op jit(solution)/shard_map/all_gather | solution.py:229
  77.8 7.2 %fusion.1 = bf16[32,640]{1,0:T(8,128)(2,1)S(1)} fusion(bf16[8192,64]{1,0:T(8,128)(2,1)} %copy.154, bf16[8192,64]{1,0:T(8,128)(2,1)S(1)} %copy.153, bf16[8192,512]{1,0:T(8,128)(2,1)} %param.21, bf16[32,1,8192]{2,1,0:T(2,128)(2,1)S(1)} %all_gather.6), kind=kOutput, calls=%fused_computation.14 | convolution fusion | flops 367001600 | bytes 11051008 | tf_op jit(solution)/shard_map/dot_general | solution.py:230
  85.0 2.8 fusion
  87.8 0.6 gather_fusion.4
  88.5 0.5 broadcast.561
  88.9 0.6 reduce.24
  89.5 0.6 reshape.1007
  90.2 4.3 scatter_custom_fusion.1
  94.5 4.6 all-to-all-start.2
  99.1 0.6 gather_fusion.5
  99.8 0.6 reduce.25
  100.3 0.6 reshape.1005
  101.0 4.8 %all-to-all-done.2 = bf16[16,2,640]{2,1,0:T(2,128)(2,1)S(1)} async-done(((bf16[16,2,640]{2,1,0:T(2,128)(2,1)}), bf16[16,2,640]{2,1,0:T(2,128)(2,1)S(1)}, u32[]{:S(2)}, u32[]{:S(2)}) %all-to-all-start.2) | async-done | bytes 40992 | tf_op jit(solution)/shard_map/all_to_all | solution.py:235
  105.8 3.5 all-to-all-start.4
  109.4 5.0 %gather_fusion.1 = bf16[128,8,2048]{2,1,0:T(8,128)(2,1)} fusion(bf16[128,8,2048]{2,1,0:T(8,128)(2,1)} %param.25, s32[1024]{0:T(1024)S(1)} %pad_clamp_fusion.3), kind=kCustom, calls=%fused_computation.1 | custom fusion | bytes 8389120 | tf_op jit(solution)/shard_map/gather | solution.py:97
  114.3 1.6 all-to-all-done.4
  116.0 4.7 all-to-all-start.1
  120.8 0.6 gather_fusion.2
  121.5 0.6 gather_fusion.3
  122.1 0.6 dynamic-slice.26
  123.6 0.5 broadcast.560
  124.1 0.7 reduce.22
  127.1 71.0 %all-to-all-done.1 = bf16[16,8,8,2048]{3,2,1,0:T(8,128)(2,1)} async-done(((bf16[16,8,8,2048]{3,2,1,0:T(8,128)(2,1)}), bf16[16,8,8,2048]{3,2,1,0:T(8,128)(2,1)}, u32[]{:S(2)}, u32[]{:S(2)}) %all-to-all-start.1) | async-done | bytes 4194336 | tf_op jit(solution)/shard_map/all_to_all | solution.py:101
  198.4 12.8 %scatter_fusion = bf16[64,8,2048]{2,1,0:T(8,128)(2,1)S(1)} fusion(bf16[64,8,2048]{2,1,0:T(8,128)(2,1)S(1)} %broadcast_in_dim.163, s32[128]{0:T(128)S(1)} %fusion.66, bf16[128,8,2048]{2,1,0:T(8,128)(2,1)} %bitcast.7), kind=kCustom, calls=%fused_computation.8 | custom fusion | bytes 12583424 | tf_op jit(solution)/shard_map/scatter | solution.py:114
  211.1 0.6 copy.191
  211.8 0.4 fusion.86
  212.1 0.5 fusion.91
  212.6 0.5 fusion.93
  213.5 0.3 fusion.19
  214.1 6.8 %copy.163 = bf16[2,1,8192]{0,1,2:T(2,128)(2,1)} copy(bf16[2,1,8192]{2,0,1:T(2,128)(2,1)S(1)} %convert_element_type.220) | data formatting | bytes 65536 | tf_op jit(solution)/shard_map/convert_element_type | solution.py:179
  220.9 45.1 %reduce.27 = bf16[8192,2]{1,0:T(8,128)(2,1)S(1)} reduce(bf16[8192,1,2]{2,1,0:T(2,128)(2,1)} %bitcast.189, bf16[]{:T(256)} %broadcast.561), dimensions={1}, to_apply=%bitcast.169.reduce_sub_computation | reduce | bytes 65538
  266.0 3.9 reshape.1011
  269.9 19.6 %all-to-all-start.3 = ((bf16[16,2,512]{2,1,0:T(2,128)(2,1)}), bf16[16,2,512]{2,1,0:T(2,128)(2,1)S(1)}, u32[]{:S(2)}, u32[]{:S(2)}) async-start(bf16[16,2,512]{2,1,0:T(2,128)(2,1)} %reshape.1011), calls=%async_computation.3 | async-start | bytes 65536 | tf_op jit(solution)/shard_map/all_to_all | solution.py:269
  289.7 0.3 fusion.18
  290.3 6.8 %copy.172 = bf16[2,1,8192]{0,1,2:T(2,128)(2,1)} copy(bf16[2,1,8192]{2,0,1:T(2,128)(2,1)S(1)} %convert_element_type.232) | data formatting | bytes 65536 | tf_op jit(solution)/shard_map/convert_element_type | solution.py:179
  297.1 45.1 %reduce.26 = bf16[8192,2]{1,0:T(8,128)(2,1)S(1)} reduce(bf16[8192,1,2]{2,1,0:T(2,128)(2,1)} %bitcast.188, bf16[]{:T(256)} %broadcast.561), dimensions={1}, to_apply=%bitcast.167.reduce_sub_computation | reduce | bytes 65538
  342.2 3.9 reshape.1009
  346.1 6.0 %all-to-all-start.5 = ((bf16[16,2,512]{2,1,0:T(2,128)(2,1)}), bf16[16,2,512]{2,1,0:T(2,128)(2,1)S(1)}, u32[]{:S(2)}, u32[]{:S(2)}) async-start(bf16[16,2,512]{2,1,0:T(2,128)(2,1)} %reshape.1009), calls=%async_computation.5 | async-start | bytes 65536 | tf_op jit(solution)/shard_map/all_to_all | solution.py:269
  352.1 8.4 %reshape.1012 = bf16[8192,1,2]{2,1,0:T(2,128)(2,1)} reshape(bf16[16,2,512]{2,1,0:T(2,128)(2,1)S(1)} %all-to-all-done.3) | data formatting | bytes 65536
  360.5 8.1 %copy.164 = bf16[2,1,8192]{2,0,1:T(2,128)(2,1)S(1)} copy(bf16[2,1,8192]{0,1,2:T(2,128)(2,1)} %bitcast.190) | data formatting | bytes 65536 | tf_op jit(solution)/shard_map/all_to_all | solution.py:269
  368.7 5.0 %convolution_bitcast_fusion.1 = f32[32,1,8192]{2,0,1:T(8,128)S(1)} fusion(bf16[32,512]{1,0:T(8,128)(2,1)S(1)} %reshape.872, bf16[512,8192]{1,0:T(8,128)(2,1)} %param.24), kind=kOutput, calls=%fused_computation.12 | convolution fusion | flops 268435456 | bytes 9469952 | tf_op jit(solution)/shard_map/dot_general | solution.py:272
  373.7 8.4 %reshape.1010 = bf16[8192,1,2]{2,1,0:T(2,128)(2,1)} reshape(bf16[16,2,512]{2,1,0:T(2,128)(2,1)S(1)} %all-to-all-done.5) | data formatting | bytes 65536
  382.1 8.1 %copy.173 = bf16[2,1,8192]{2,0,1:T(2,128)(2,1)S(1)} copy(bf16[2,1,8192]{0,1,2:T(2,128)(2,1)} %bitcast.191) | data formatting | bytes 65536 | tf_op jit(solution)/shard_map/all_to_all | solution.py:269
  390.3 5.0 %convolution_bitcast_fusion = f32[32,1,8192]{2,0,1:T(8,128)S(1)} fusion(bf16[32,512]{1,0:T(8,128)(2,1)S(1)} %reshape.878, bf16[512,8192]{1,0:T(8,128)(2,1)} %param.24), kind=kOutput, calls=%fused_computation.11 | convolution fusion | flops 268435456 | bytes 9469952 | tf_op jit(solution)/shard_map/dot_general | solution.py:272
  395.2 75.8 %all-reduce.6 = (bf16[32,1,8192]{2,0,1:T(8,128)(2,1)S(1)}, bf16[32,1,8192]{2,0,1:T(8,128)(2,1)S(1)}) all-reduce(f32[32,1,8192]{2,0,1:T(8,128)S(1)} %convolution_bitcast_fusion, f32[32,1,8192]{2,0,1:T(8,128)S(1)} %convolution_bitcast_fusion.1), channel_id=3, replica_groups=mesh['rep'=2,'cand'=16] {'cand'}, use_global_device_ids=true, to_apply=%region_18.19.clone | all-reduce | flops 524288 | bytes 3145728
  471.2 0.7 copy.175
  (113 shorter events, 5.5 us)
Async XLA Ops:
  0.6 120.8 %copy-start = (s32[64]{0:T(128)S(1)}, s32[64]{0:T(128)}, u32[]{:S(2)}) copy-start(s32[64]{0:T(128)} %param.29) | copy-start | bytes 772
  16.6 77.9 %all-to-all-start = ((s32[16,1,8]{2,1,0:T(1,128)}), s32[16,1,8]{2,1,0:T(1,128)S(1)}, u32[]{:S(2)}, u32[]{:S(2)}) async-start(s32[16,1,8]{2,1,0:T(1,128)} %bitcast.4), calls=%async_computation | async-start | bytes 16384 | tf_op jit(solution)/shard_map/all_to_all | solution.py:102
  57.0 28.0 %slice-start = ((s8[8388608]{0:T(1024)(128)(4,1)}), s8[4194304]{0:T(1024)(128)(4,1)S(1)}, s32[]{:S(2)}) async-start(s8[8388608]{0:T(1024)(128)(4,1)} %bitcast.210), calls=%async_computation.6 | async-start | bytes 8388608
  77.8 7.2 %copy-start.4 = (bf16[8192,64]{1,0:T(8,128)(2,1)S(1)}, bf16[8192,64]{1,0:T(8,128)(2,1)}, u32[]{:S(2)}) copy-start(bf16[8192,64]{1,0:T(8,128)(2,1)} %copy.154) | copy-start | bytes 3145732
  77.8 7.2 %slice-start.1 = ((s8[8388608]{0:T(1024)(128)(4,1)}), s8[4194304]{0:T(1024)(128)(4,1)S(1)}, s32[]{:S(2)}) async-start(s8[8388608]{0:T(1024)(128)(4,1)} %bitcast.210), calls=%async_computation.7 | async-start | bytes 8388608
  94.5 11.3 %all-to-all-start.2 = ((bf16[16,2,640]{2,1,0:T(2,128)(2,1)}), bf16[16,2,640]{2,1,0:T(2,128)(2,1)S(1)}, u32[]{:S(2)}, u32[]{:S(2)}) async-start(bf16[16,2,640]{2,1,0:T(2,128)(2,1)} %reshape.1007), calls=%async_computation.2 | async-start | bytes 81920 | tf_op jit(solution)/shard_map/all_to_all | solution.py:235
  105.8 10.2 %all-to-all-start.4 = ((bf16[16,2,640]{2,1,0:T(2,128)(2,1)}), bf16[16,2,640]{2,1,0:T(2,128)(2,1)S(1)}, u32[]{:S(2)}, u32[]{:S(2)}) async-start(bf16[16,2,640]{2,1,0:T(2,128)(2,1)} %reshape.1005), calls=%async_computation.4 | async-start | bytes 81920 | tf_op jit(solution)/shard_map/all_to_all | solution.py:235
  109.3 11.5 %copy-start.2 = (s32[32]{0:T(128)S(1)}, s32[32]{0:T(128)}, u32[]{:S(2)}) copy-start(s32[32]{0:T(128)} %param.26) | copy-start | bytes 388
  109.3 12.8 %copy-start.5 = (u32[32]{0:T(128)S(1)}, u32[32]{0:T(128)}, u32[]{:S(2)}) copy-start(u32[32]{0:T(128)} %constant.193) | copy-start | bytes 388
  116.0 82.1 %all-to-all-start.1 = ((bf16[16,8,8,2048]{3,2,1,0:T(8,128)(2,1)}), bf16[16,8,8,2048]{3,2,1,0:T(8,128)(2,1)}, u32[]{:S(2)}, u32[]{:S(2)}) async-start(bf16[16,8,8,2048]{3,2,1,0:T(8,128)(2,1)} %bitcast.187), calls=%async_computation.1 | async-start | bytes 8388608 | tf_op jit(solution)/shard_map/all_to_all | solution.py:101
  211.1 9.8 %copy-start.3 = (bf16[64,8,2048]{2,1,0:T(8,128)(2,1)}, bf16[64,8,2048]{2,1,0:T(8,128)(2,1)S(1)}, u32[]{:S(2)}) copy-start(bf16[64,8,2048]{2,1,0:T(8,128)(2,1)S(1)} %scatter_fusion) | copy-start | bytes 6291460
  269.9 76.2 %all-to-all-start.3 = ((bf16[16,2,512]{2,1,0:T(2,128)(2,1)}), bf16[16,2,512]{2,1,0:T(2,128)(2,1)S(1)}, u32[]{:S(2)}, u32[]{:S(2)}) async-start(bf16[16,2,512]{2,1,0:T(2,128)(2,1)} %reshape.1011), calls=%async_computation.3 | async-start | bytes 65536 | tf_op jit(solution)/shard_map/all_to_all | solution.py:269
  346.1 27.5 %all-to-all-start.5 = ((bf16[16,2,512]{2,1,0:T(2,128)(2,1)}), bf16[16,2,512]{2,1,0:T(2,128)(2,1)S(1)}, u32[]{:S(2)}, u32[]{:S(2)}) async-start(bf16[16,2,512]{2,1,0:T(2,128)(2,1)} %reshape.1009), calls=%async_computation.5 | async-start | bytes 65536 | tf_op jit(solution)/shard_map/all_to_all | solution.py:269
  382.1 89.9 %copy-start.1 = (s32[64]{0:T(128)S(1)}, s32[64]{0:T(128)}, u32[]{:S(2)}) copy-start(s32[64]{0:T(128)} %param.29) | copy-start | bytes 772
where the time goes:
time: 474 us; the launch traced here: 472 us
  blocking collectives  121 us (26%)
  other arithmetic  104 us (22%)
  local copies, waits for them, and re-layouts  99 us (21%)
  waiting for transfers between devices  77.5 us (16%)
  starting transfers between devices  45.9 us (10%)
  matrix products  22.5 us (5%)
    unnamed x3, other arithmetic  90.3 us
    unnamed x1, blocking collectives  75.8 us
    all_to_all x1, waiting for transfers between devices, relocate_pages(): lax.all_to_all(outgoing, 'cand', split_axis=0, concat_axis=0, tiled=True)  71 us
    all_gather x2, blocking collectives, body(): block_rows = lax.all_gather(token_rows, 'cand', axis=0, tiled=True)  45.5 us
    unnamed x32, local copies, waits for them, and re-layouts  33.4 us
    all_to_all x2, starting transfers between devices, body(): lax.all_to_all(combined_channels, 'cand', split_axis=2, concat_axis=0, ti...  25.6 us
    all_to_all x4, local copies, waits for them, and re-layouts, body(): lax.all_to_all(combined_channels, 'cand', split_axis=2, concat_axis=0, ti...  16.2 us
    convert_element_type x4, local copies, waits for them, and re-layouts, attend(): return combined_channels.reshape(total_row_count, token_pair_group, ASKER...  13.6 us
  transfers between devices with their start and end apart: 6, of which 3 were waited for; matrix products, arithmetic and copies ran while one was open for 24% of the time, Pallas kernels for 0%

commit v1 on v0

v1 whole, which is shorter than its diff:
```python
import functools
import math

import jax
import jax.numpy as jnp
import numpy as np
from jax import lax
from jax.experimental import pallas as pl
from jax.experimental.pallas import tpu as pltpu
from jax.sharding import PartitionSpec as P

ASKER_UNITS = 64
KV_ATTN_UNITS = 8
ATTN_DIM = 128


EPS = 1e-06
ROPE_BASE = 1000000.0
NEG_FILL = -1e30


def spot_numbering(winner_chip_assignment, per_device):
    position_vector = jnp.arange(winner_chip_assignment.shape[0], dtype=jnp.int32)
    earlier = position_vector[None, :] < position_vector[:, None]
    same_dev = winner_chip_assignment[None, :] == winner_chip_assignment[:, None]
    position_on_chip = jnp.sum(jnp.where(earlier & same_dev, 1, 0), axis=1).astype(jnp.int32)
    return winner_chip_assignment * per_device + position_on_chip


def normalize(row_block, entry_scaling_factor):
    rows_f32 = row_block.astype(jnp.float32)
    mean_sq = jnp.mean(rows_f32 * rows_f32, axis=-1, keepdims=True)
    return (rows_f32 * lax.rsqrt(mean_sq + EPS) * entry_scaling_factor.astype(jnp.float32)).astype(
        jnp.bfloat16
    )


def rotate(vectors, positions):
    half_dim = vectors.shape[-1] // 2
    frequencies = ROPE_BASE ** (
        -(jnp.arange(half_dim, dtype=jnp.float32) * 2.0 / vectors.shape[-1])
    )
    angles = positions.astype(jnp.float32)[..., None] * frequencies
    cosine_table = jnp.cos(angles)[..., None, :]
    sine_table = jnp.sin(angles)[..., None, :]
    first_half = vectors[..., :half_dim]
    second_half = vectors[..., half_dim:]
    return jnp.concatenate(
        [
            first_half * cosine_table - second_half * sine_table,
            second_half * cosine_table + first_half * sine_table,
        ],
        axis=-1,
    )


ROWS = 16
MESH = pl.DeviceIdType.MESH
BF = jnp.bfloat16
F32 = jnp.float32


def place(z, y, core):
    return (z * 2 + y) * 2 + core


def remote(src, dst, send_sem, recv_sem, device):
    return pltpu.make_async_remote_copy(
        src_ref=src,
        dst_ref=dst,
        send_sem=send_sem,
        recv_sem=recv_sem,
        device_id={"cand": device},
        device_id_type=MESH,
    )


def greet_all(n, me):
    barrier = pltpu.get_barrier_semaphore()

    @pl.loop(1, n)
    def _(k):
        pl.semaphore_signal(
            barrier, inc=1, device_id={"cand": lax.rem(me + k, n)}, device_id_type=MESH
        )

    pl.semaphore_wait(barrier, n - 1)


class Gather:
    def __init__(self, n, me, own, buf, base, ss, rs):
        self.nz = n // 4
        self.core = lax.rem(me, 2)
        self.y = lax.rem(me // 2, 2)
        self.z = me // 4
        self.me, self.own, self.buf, self.base, self.ss, self.rs = me, own, buf, base, ss, rs

    def copy(self, src, block, level, k, device):
        dst = self.buf.at[self.base + block]
        return remote(
            dst if src is None else src, dst, self.ss.at[level, k], self.rs.at[level, k], device
        )

    def block(self, k, other_y, other_core):
        z = lax.rem(self.z - k + self.nz, self.nz)
        y = 1 - self.y if other_y else self.y
        core = 1 - self.core if other_core else self.core
        return place(z, y, core)

    def along_z(self, k):
        device = place(lax.rem(self.z + k, self.nz), self.y, self.core)
        return self.copy(self.own, self.me, 0, k, device)

    def across_y(self, k):
        device = place(self.z, 1 - self.y, self.core)
        return self.copy(None, self.block(k, False, False), 1, k, device)

    def across_core(self, k, other_y):
        device = place(self.z, self.y, 1 - self.core)
        return self.copy(
            None, self.block(k, other_y, False), 2, k + (self.nz if other_y else 0), device
        )

    def start(self):
        @pl.loop(1, self.nz)
        def _(k):
            self.along_z(k).start()

    def finish(self):
        self.across_y(0).start()
        self.across_core(0, False).start()

        @pl.loop(1, self.nz)
        def _(k):
            self.copy(None, self.block(k, False, False), 0, k, self.me).wait_recv()
            self.across_y(k).start()
            self.across_core(k, False).start()

        @pl.loop(0, self.nz)
        def _(k):
            self.copy(None, self.block(k, True, False), 1, k, self.me).wait_recv()
            self.across_core(k, True).start()

        @pl.loop(0, self.nz)
        def _(k):
            self.copy(None, self.block(k, False, True), 2, k, self.me).wait_recv()
            self.copy(None, self.block(k, True, True), 2, k + self.nz, self.me).wait_recv()

    def drain(self):
        @pl.loop(1, self.nz)
        def _(k):
            self.along_z(k).wait_send()

        @pl.loop(0, self.nz)
        def _(k):
            self.across_y(k).wait_send()
            self.across_core(k, False).wait_send()
            self.across_core(k, True).wait_send()


def move_kernel(
    n, heads, pick, spread, x, send, wq_hbm, wk_hbm, wv_hbm, pages, qkv,
    xall, wq, wk, wv, outq, local,
    x_ss, x_rs, o_ss, o_rs, p_ss, p_rs, q_ss, q_rs,
):
    me = lax.axis_index("cand")
    loads = [
        pltpu.make_async_copy(a, b, local.at[i])
        for i, (a, b) in enumerate(((wq_hbm, wq), (wk_hbm, wk), (wv_hbm, wv)))
    ]
    for load in loads:
        load.start()
    own_page = pltpu.make_async_copy(send.at[me], pages.at[me], local.at[3])
    own_extra = pltpu.make_async_copy(send.at[n], pages.at[n + me], local.at[4])
    own_page.start()
    own_extra.start()
    xall[me] = x[...]
    greet_all(n, me)
    rows = Gather(n, me, x, xall, 0, x_ss, x_rs)
    extra = Gather(n, me, send.at[n], pages, n, o_ss, o_rs)
    rows.start()
    extra.start()

    def page_copy(k):
        device = lax.rem(me + k, n)
        return remote(send.at[device], pages.at[me], p_ss.at[k], p_rs.at[k], device)

    @pl.loop(1, n)
    def _(k):
        page_copy(k).start()

    rows.finish()
    for load in loads:
        load.wait()
    flat = xall[...].reshape(n * ROWS, xall.shape[2])
    depth = xall.shape[2]
    q_sum = jnp.zeros((n * 4, wq.shape[1]), F32)
    k_sum = jnp.zeros((n * 4, wk.shape[1]), F32)
    v_sum = jnp.zeros((n * 4, wv.shape[1]), F32)
    for c in range(4):
        xc = jnp.dot(pick[c], flat, preferred_element_type=F32).astype(BF)
        part = pl.ds(c * depth, depth)
        q_sum += jnp.dot(xc, wq[part, :], preferred_element_type=F32)
        k_sum += jnp.dot(xc, wk[part, :], preferred_element_type=F32)
        v_sum += jnp.dot(xc, wv[part, :], preferred_element_type=F32)
    q16 = q_sum.astype(BF)
    slab = jnp.zeros((n * ROWS, ATTN_DIM), F32)
    for h in range(heads):
        slab += jnp.dot(
            spread[h], q16[:, h * ATTN_DIM : (h + 1) * ATTN_DIM], preferred_element_type=F32
        )
    pad = ATTN_DIM - wk.shape[1] - wv.shape[1]
    parts = [k_sum, v_sum] + ([jnp.zeros((n * 4, pad), F32)] if pad else [])
    kv16 = jnp.concatenate(parts, axis=1).astype(BF)
    kv_slab = jnp.dot(spread[0], kv16, preferred_element_type=F32)
    outq[:, :ROWS, :] = slab.astype(BF).reshape(n, ROWS, ATTN_DIM)
    outq[:, ROWS:, :] = kv_slab.astype(BF).reshape(n, ROWS, ATTN_DIM)
    own_q = pltpu.make_async_copy(outq.at[me], qkv.at[me], local.at[5])
    own_q.start()

    def q_copy(k):
        device = lax.rem(me + k, n)
        return remote(outq.at[device], qkv.at[me], q_ss.at[k], q_rs.at[k], device)

    @pl.loop(1, n)
    def _(k):
        q_copy(k).start()

    own_extra.wait()
    extra.finish()

    @pl.loop(1, n)
    def _(k):
        source = lax.rem(me - k + n, n)
        remote(send.at[0], pages.at[source], p_ss.at[k], p_rs.at[k], me).wait_recv()
        remote(outq.at[0], qkv.at[source], q_ss.at[k], q_rs.at[k], me).wait_recv()

    rows.drain()
    extra.drain()

    @pl.loop(1, n)
    def _(k):
        page_copy(k).wait_send()
        q_copy(k).wait_send()

    own_page.wait()
    own_q.wait()


def attend_kernel(
    n, heads, where_from, extents, pages, q, cos, sin, k_new, v_new, moved, mixed,
    held, scores, sems, out_sem,
):
    count = held.shape[0]

    def page_copy(i):
        return pltpu.make_async_copy(pages.at[where_from[i]], held.at[i], sems.at[i])

    @pl.loop(0, count)
    def _(i):
        page_copy(i).start()

    slabs = KV_ATTN_UNITS // heads
    rows = slabs * ROWS
    context = count * held.shape[1]
    half = context // 2
    row_c = lax.broadcasted_iota(jnp.int32, (rows, context), 0)
    col_c = lax.broadcasted_iota(jnp.int32, (rows, context), 1)
    survivor = (row_c % 4) // 2
    extent = jnp.where(survivor == 0, extents[0], extents[1])
    at = col_c - survivor * half
    valid_c = (at >= 0) & (at < extent)
    row_f = lax.broadcasted_iota(jnp.int32, (rows, ROWS), 0) % 4
    col_f = lax.broadcasted_iota(jnp.int32, (rows, ROWS), 1)
    valid_f = (col_f // 2 == row_f // 2) & (col_f % 2 <= row_f % 2) & (col_f < 4)
    scale = 1.0 / math.sqrt(ATTN_DIM)
    contract = (((1,), (1,)), ((), ()))

    @pl.loop(0, count)
    def _(i):
        page_copy(i).wait()

    out = pltpu.make_async_copy(held, moved, out_sem)
    out.start()
    for g in range(KV_ATTN_UNITS):
        qg = q[g * slabs : (g + 1) * slabs, :ROWS, :].astype(F32)
        qg = qg * cos[...][None] + pltpu.roll(qg, ATTN_DIM // 2, 2) * sin[...][None]
        qg = qg.reshape(rows, ATTN_DIM).astype(BF)
        lanes = pl.ds(g * ATTN_DIM, ATTN_DIM)
        keys = held[:, :, lanes].astype(F32).reshape(context, ATTN_DIM).astype(BF)
        lanes = pl.ds((KV_ATTN_UNITS + g) * ATTN_DIM, ATTN_DIM)
        values = held[:, :, lanes].astype(F32).reshape(context, ATTN_DIM).astype(BF)
        s_c = lax.dot_general(qg, keys, contract, preferred_element_type=F32) * scale
        s_f = lax.dot_general(qg, k_new[g], contract, preferred_element_type=F32) * scale
        s_c = jnp.where(valid_c, s_c, NEG_FILL)
        s_f = jnp.where(valid_f, s_f, NEG_FILL)
        peak = jnp.maximum(
            jnp.max(s_c, axis=-1, keepdims=True), jnp.max(s_f, axis=-1, keepdims=True)
        )
        e_c = jnp.where(valid_c, jnp.exp(s_c - peak), 0.0)
        e_f = jnp.where(valid_f, jnp.exp(s_f - peak), 0.0)
        total = jnp.sum(e_c, axis=-1, keepdims=True) + jnp.sum(e_f, axis=-1, keepdims=True)
        w_c = (e_c / total).astype(BF)
        w_f = (e_f / total).astype(BF)
        o = jnp.dot(w_c, values, preferred_element_type=F32)
        o += jnp.dot(w_f, v_new[g], preferred_element_type=F32)
        mixed[g * slabs : (g + 1) * slabs] = o.astype(BF).reshape(slabs, ROWS, ATTN_DIM)
    out.wait()


def project_kernel(
    n, heads, chunks, squeeze, mixed, wf_hbm, result,
    wf, gathered, partial, from_core, from_y, to_z, from_z, local,
    m_ss, m_rs, c_ss, c_rs, y_ss, y_rs, z_ss, z_rs,
):
    me = lax.axis_index("cand")
    nz = n // 4
    core, y, z = lax.rem(me, 2), lax.rem(me // 2, 2), me // 4
    load = pltpu.make_async_copy(wf_hbm, wf, local.at[0])
    load.start()
    gathered[me] = mixed[me]
    greet_all(n, me)

    def m_copy(k):
        device = lax.rem(me + k, n)
        return remote(mixed.at[device], gathered.at[me], m_ss.at[k], m_rs.at[k], device)

    @pl.loop(1, n)
    def _(k):
        m_copy(k).start()

    @pl.loop(1, n)
    def _(k):
        source = lax.rem(me - k + n, n)
        remote(mixed.at[0], gathered.at[source], m_ss.at[k], m_rs.at[k], me).wait_recv()

    flat = gathered[...].reshape(n * ROWS, ATTN_DIM)
    ordered = jnp.concatenate(
        [
            jnp.dot(squeeze[h], flat, preferred_element_type=F32).astype(BF)
            for h in range(heads)
        ],
        axis=1,
    )
    load.wait()
    width = wf.shape[1] // chunks

    def c_copy(i):
        return remote(
            partial.at[i, 1 - core], from_core.at[i], c_ss.at[i], c_rs.at[i], place(z, y, 1 - core)
        )

    def y_copy(i):
        return remote(
            partial.at[i, core, 1 - y], from_y.at[i], y_ss.at[i], y_rs.at[i],
            place(z, 1 - y, core),
        )

    def z_copy(i, k):
        other = lax.rem(z + k, nz)
        return remote(
            to_z.at[i, other], from_z.at[i, k], z_ss.at[i, k], z_rs.at[i, k],
            place(other, y, core),
        )

    for i in range(chunks):
        product = jnp.dot(
            ordered, wf[:, i * width : (i + 1) * width], preferred_element_type=F32
        )
        partial[i] = product.reshape(2, 2, nz * 4, width)
        c_copy(i).start()
    for i in range(chunks):
        c_copy(i).wait_recv()
        partial[i, core] = partial[i, core] + from_core[i]
        y_copy(i).start()
    for i in range(chunks):
        y_copy(i).wait_recv()
        total = partial[i, core, y] + from_y[i]
        for other in range(nz):
            to_z[i, other] = total[other * 4 : (other + 1) * 4, :]

        @pl.loop(1, nz)
        def _(k):
            z_copy(i, k).start()

    for i in range(chunks):
        total = to_z[i, z]
        for k in range(1, nz):
            z_copy(i, k).wait_recv()
            total = total + from_z[i, k]
        result[:, i * width : (i + 1) * width] = total.astype(BF)

    @pl.loop(1, n)
    def _(k):
        m_copy(k).wait_send()

    for i in range(chunks):
        c_copy(i).wait_send()
        y_copy(i).wait_send()

        @pl.loop(1, nz)
        def _(k):
            z_copy(i, k).wait_send()


def body(
    layer_activations,
    entry_scaling_factor,
    asker_matrix,
    address_matrix,
    content_matrix,
    final_matrix,
    candidate_memory_blocks,
    winning_candidates,
    winner_chip_assignment,
    candidate_block_map,
    candidate_filled_extent,
):
    n = lax.axis_size("cand")
    me = lax.axis_index("cand")
    nz = n // 4
    kept, tokens, embed = layer_activations.shape
    spots, page, page_width = candidate_memory_blocks.shape
    chain = candidate_block_map.shape[1]
    count = kept * chain
    share = count // n
    heads = asker_matrix.shape[1] // ATTN_DIM
    key_cols = address_matrix.shape[1]
    group_rows = kept * tokens

    slot = spot_numbering(winner_chip_assignment, kept)
    order = jnp.arange(slot.shape[0], dtype=jnp.int32)
    in_slot = slot[None, :] == order[:, None]
    keep = jnp.sum(jnp.where(in_slot, order[None, :], 0), axis=1)
    candidate = jnp.sum(jnp.where(in_slot, winning_candidates[None, :], 0), axis=1)
    table = candidate_block_map[candidate].reshape(n, count)
    extents = lax.dynamic_slice_in_dim(candidate_filled_extent[candidate], me * kept, kept)
    spot_ids = jnp.arange(count, dtype=jnp.int32)
    before = spot_ids[None, :] < spot_ids[:, None]
    mine = table // spots == me
    rank = jnp.sum(jnp.where(mine[:, None, :] & before[None], 1, 0), axis=2)
    ranks = jnp.arange(2 * share, dtype=jnp.int32)
    chosen = mine[:, None, :] & (rank[:, None, :] == ranks[None, :, None])
    sent = jnp.sum(jnp.where(chosen, (table % spots)[:, None, :], 0), axis=2)
    sent = jnp.concatenate(
        [sent[:, :share], jnp.sum(sent[:, share:], axis=0, keepdims=True)], axis=0
    )
    send = candidate_memory_blocks[sent.reshape(-1)].reshape(n + 1, share, page, page_width)
    arriving = lax.dynamic_slice_in_dim(table, me, 1)[0] // spots
    arrived_rank = jnp.sum(
        jnp.where((arriving[:, None] == arriving[None, :]) & before, 1, 0), axis=1
    )
    where_from = jnp.where(
        arrived_rank < share,
        arriving * share + arrived_rank,
        (n + arriving - 1) * share + arrived_rank,
    )

    x = normalize(layer_activations, entry_scaling_factor)
    pieces = ROWS // group_rows
    x = (
        x.reshape(group_rows, pieces, embed // pieces)
        .transpose(1, 0, 2)
        .reshape(ROWS, embed // pieces)
    )
    col = np.arange(n * ROWS)
    source_row = (col // ROWS) * group_rows + col % group_rows
    piece = (col // group_rows) % pieces
    wanted = (keep[:, None] * tokens + jnp.arange(tokens, dtype=jnp.int32)).reshape(-1)
    pick = jnp.where(
        (wanted[None, :, None] == source_row[None, None, :])
        & (np.arange(pieces)[:, None, None] == piece[None, None, :]),
        1.0,
        0.0,
    ).astype(BF)
    row = np.arange(n * group_rows)
    spread = np.stack(
        [(row[None, :] == source_row[:, None]) & (piece[:, None] == h) for h in range(pieces)]
    )
    by_level = (
        row.reshape(nz, 2, 2, group_rows).transpose(2, 1, 0, 3).reshape(-1)
    )
    squeeze = np.stack(
        [
            (by_level[:, None] == source_row[None, :]) & (piece[None, :] == h)
            for h in range(heads)
        ]
    )
    spread = jnp.asarray(spread.astype(jnp.bfloat16))
    squeeze = jnp.asarray(squeeze.astype(jnp.bfloat16))

    any_space = pl.BlockSpec(memory_space=pl.ANY)
    vmem = pl.BlockSpec(memory_space=pltpu.VMEM)
    smem = pl.BlockSpec(memory_space=pltpu.SMEM)
    dma = pltpu.SemaphoreType.DMA
    pages, qkv = pl.pallas_call(
        functools.partial(move_kernel, n, heads),
        out_shape=(
            jax.ShapeDtypeStruct((2 * n, share, page, page_width), BF),
            jax.ShapeDtypeStruct((n, 2 * ROWS, ATTN_DIM), BF),
        ),
        in_specs=[vmem, vmem, vmem] + [any_space] * 4,
        out_specs=(any_space, any_space),
        scratch_shapes=[
            pltpu.VMEM((n, ROWS, embed // pieces), BF),
            pltpu.VMEM(asker_matrix.shape, BF),
            pltpu.VMEM(address_matrix.shape, BF),
            pltpu.VMEM(content_matrix.shape, BF),
            pltpu.VMEM((n, 2 * ROWS, ATTN_DIM), BF),
            dma((6,)),
            dma((3, 2 * nz)),
            dma((3, 2 * nz)),
            dma((3, 2 * nz)),
            dma((3, 2 * nz)),
            dma((n,)),
            dma((n,)),
            dma((n,)),
            dma((n,)),
        ],
        compiler_params=pltpu.CompilerParams(
            collective_id=0, has_side_effects=True, vmem_limit_bytes=48 << 20
        ),
        name="move_and_project",
    )(pick, spread, x, send, asker_matrix, address_matrix, content_matrix)

    positions = extents[:, None] + jnp.arange(tokens, dtype=jnp.int32)[None, :]
    frequencies = ROPE_BASE ** (
        -(jnp.arange(ATTN_DIM // 2, dtype=jnp.float32) * 2.0 / ATTN_DIM)
    )
    angles = positions.reshape(-1).astype(F32)[:, None] * frequencies
    cosine, sine = jnp.cos(angles), jnp.sin(angles)
    cosine = jnp.concatenate([cosine, cosine], axis=1)
    sine = jnp.concatenate([-sine, sine], axis=1)
    fresh = qkv[:, ROWS : ROWS + group_rows, :]
    k_new = fresh[:, :, :key_cols].transpose(1, 0, 2).reshape(group_rows, KV_ATTN_UNITS, ATTN_DIM)
    v_new = fresh[:, :, key_cols : 2 * key_cols].transpose(1, 0, 2)
    v_new = v_new.reshape(group_rows, KV_ATTN_UNITS, ATTN_DIM)
    k_new = rotate(
        k_new.astype(F32).reshape(kept, tokens, KV_ATTN_UNITS, ATTN_DIM), positions
    ).astype(BF)
    k_new = k_new.reshape(group_rows, KV_ATTN_UNITS, ATTN_DIM).transpose(1, 0, 2)
    v_new = v_new.transpose(1, 0, 2)
    tall = ((0, 0), (0, ROWS - group_rows), (0, 0))
    k_new, v_new = jnp.pad(k_new, tall), jnp.pad(v_new, tall)

    moved, mixed = pl.pallas_call(
        functools.partial(attend_kernel, n, heads),
        out_shape=(
            jax.ShapeDtypeStruct((count, page, page_width), BF),
            jax.ShapeDtypeStruct((n, ROWS, ATTN_DIM), BF),
        ),
        in_specs=[smem, smem, any_space, vmem, vmem, vmem, vmem, vmem],
        out_specs=(any_space, vmem),
        scratch_shapes=[
            pltpu.VMEM((count, page, page_width), BF),
            pltpu.VMEM((8, 128), F32),
            dma((count,)),
            dma,
        ],
        compiler_params=pltpu.CompilerParams(vmem_limit_bytes=32 << 20),
        name="attend",
    )(
        where_from,
        extents,
        pages.reshape(2 * n * share, page, page_width),
        qkv,
        jnp.tile(cosine, (pieces, 1)),
        jnp.tile(sine, (pieces, 1)),
        k_new,
        v_new,
    )

    chunks = 4
    width = embed // chunks
    result = pl.pallas_call(
        functools.partial(project_kernel, n, heads, chunks),
        out_shape=jax.ShapeDtypeStruct((group_rows, embed), BF),
        in_specs=[vmem, vmem, any_space],
        out_specs=vmem,
        scratch_shapes=[
            pltpu.VMEM(final_matrix.shape, BF),
            pltpu.VMEM((n, ROWS, ATTN_DIM), BF),
            pltpu.VMEM((chunks, 2, 2, nz * group_rows, width), F32),
            pltpu.VMEM((chunks, 2, nz * group_rows, width), F32),
            pltpu.VMEM((chunks, nz * group_rows, width), F32),
            pltpu.VMEM((chunks, nz, group_rows, width), F32),
            pltpu.VMEM((chunks, nz, group_rows, width), F32),
            dma((1,)),
            dma((n,)),
            dma((n,)),
            dma((chunks,)),
            dma((chunks,)),
            dma((chunks,)),
            dma((chunks,)),
            dma((chunks, nz)),
            dma((chunks, nz)),
        ],
        compiler_params=pltpu.CompilerParams(
            collective_id=1, has_side_effects=True, vmem_limit_bytes=48 << 20
        ),
        name="project_and_sum",
    )(squeeze, mixed, final_matrix)
    return (
        result.reshape(kept, tokens, embed),
        moved.reshape(kept, chain, page, page_width),
    )


def solution(mesh):
    return jax.shard_map(
        body,
        mesh=mesh,
        in_specs=(
            P(("rep", "cand"), None, None),
            P(),
            P(None, "cand"),
            P(None, "cand"),
            P(None, "cand"),
            P("cand", None),
            P(("rep", "cand"), None, None),
            P("rep"),
            P("rep"),
            P("rep", None),
            P("rep"),
        ),
        out_specs=(P(("rep", "cand"), None, None), P(("rep", "cand"), None, None, None)),
        check_vma=False,
    )
```

time: 474 us -> 137 us (0.29)
  blocking collectives: 121 us -> 0 us
  Pallas kernels: 0 us -> 112 us
  other arithmetic: 104 us -> 8.34 us
  local copies, waits for them, and re-layouts: 99 us -> 15.7 us
  waiting for transfers between devices: 77.5 us -> 0 us
  starting transfers between devices: 45.9 us -> 0 us
  matrix products: 22.5 us -> 0 us
    pallas_call x0 -> x3, Pallas kernels: none -> 112 us  [the longest x1 73.4 us: body(): pl.pallas_call(functools.partial(move_kernel, n, heads), out_shape=(jax.S...]
    unnamed x3 -> x0, other arithmetic: 90.3 us -> none
    all_to_all x6 -> x0, waiting for transfers between devices: 77.5 us -> none  [the longest x1 71 us: relocate_pages(): lax.all_to_all(outgoing, 'cand', split_axis=0, concat_axis=0, tiled=True)]
    unnamed x1 -> x0, blocking collectives: 75.8 us -> none
    all_to_all x6 -> x0, starting transfers between devices: 45.9 us -> none  [the longest x2 25.6 us: body(): lax.all_to_all(combined_channels, 'cand', split_axis=2, concat_axis=0, ti...]
    all_gather x2 -> x0, blocking collectives: 45.5 us -> none  [body(): block_rows = lax.all_gather(token_rows, 'cand', axis=0, tiled=True)]
    unnamed x32 -> x15, local copies, waits for them, and re-layouts: 33.4 us -> 8.42 us
    dot_general x12 -> x0, matrix products: 22.5 us -> none  [the longest x2 9.97 us: body(): jnp.dot(block_rows.reshape(-1, block_rows.shape[2]), joined, preferred_el...]
  transfers between devices with their start and end apart: 6 -> 0, of which waited for: 3 -> 0; matrix products, arithmetic and copies ran while one was open for 24% -> 0% of each run, Pallas kernels for 0% -> 0%
where the time goes in v1:
time: 137 us; the launch traced here: 136 us
  Pallas kernels  112 us (82%)
  local copies, waits for them, and re-layouts  15.7 us (11%)
  other arithmetic  8.34 us (6%)
    pallas_call x1, Pallas kernels, body(): pl.pallas_call(functools.partial(move_kernel, n, heads), out_shape=(jax.S...  73.4 us
    pallas_call x1, Pallas kernels, body(): pl.pallas_call(functools.partial(project_kernel, n, heads, chunks), out_s...  29.2 us
    pallas_call x1, Pallas kernels, body(): pl.pallas_call(functools.partial(attend_kernel, n, heads), out_shape=(jax...  8.93 us
    unnamed x15, local copies, waits for them, and re-layouts  8.42 us
    gather x1, local copies, waits for them, and re-layouts, body(): candidate_memory_blocks[sent.reshape(-1)]  4.54 us

profile of v1, /device:TPU:0, one launch (start us, length us, event | category | flops | bytes accessed | tf_op | source)
XLA Modules:
  0.0 136.4 jit_solution(12758143690998989680)
XLA Ops:
  0.6 0.0 copy-start
  0.6 0.8 copy.41
  1.4 0.9 select_reduce_fusion.5
  2.4 0.7 multiply_add_fusion
  3.0 0.8 select_reduce_fusion.3
  3.8 0.6 gather_fusion
  4.4 0.1 reshape.298
  4.5 0.2 select_reduce_fusion.2
  4.7 0.0 copy-done
  4.7 0.7 gather_fusion.1
  5.4 0.1 dynamic_slice.7.extents
  5.5 0.1 iota_add_fusion
  5.6 0.1 add.132
  5.7 0.8 broadcast_compare_fusion
  6.5 0.7 select_convert_fusion.pick
  7.2 0.7 convert_element_type.44
  7.9 1.0 fusion
  8.9 1.0 fusion.2
  10.0 0.1 copy.52
  10.1 0.4 select_reduce_fusion
  10.5 0.3 select_reduce_fusion.1
  10.8 0.1 fusion.12
  10.9 0.1 reshape.301
  11.0 0.0 copy-start.5
  11.0 4.5 %gather_fusion.2 = bf16[68,8,2048]{2,1,0:T(8,128)(2,1)} fusion(bf16[128,8,2048]{2,1,0:T(8,128)(2,1)} %param.21, s32[1024]{0:T(1024)S(1)} %pad_clamp_fusion), kind=kCustom, calls=%fused_computation.2 | custom fusion | bytes 4456720 | tf_op jit(solution)/shard_map/gather | solution.py:448
  15.6 0.0 copy-done.5
  15.6 1.1 copy.43.wk_hbm
  16.7 0.0 copy-start.3
  16.7 2.8 %copy.44.wv_hbm = bf16[8192,64]{1,0:T(8,128)(2,1)} copy(bf16[8192,64]{0,1:T(8,128)(2,1)} %param.19) | data formatting | bytes 2097152 | tf_op args[4]
  19.4 0.0 copy-done.3
  19.4 0.0 copy-start.1
  19.4 1.6 %copy-done.1 = bf16[8192,64]{1,0:T(8,128)(2,1)S(1)} copy-done((bf16[8192,64]{1,0:T(8,128)(2,1)S(1)}, bf16[8192,64]{1,0:T(8,128)(2,1)}, u32[]{:S(2)}) %copy-start.1) | copy-done | bytes 1048600
  21.0 73.4 %move_and_project.1 = (bf16[32,4,8,2048]{3,2,1,0:T(8,128)(2,1)}, bf16[16,32,128]{2,1,0:T(8,128)(2,1)S(1)}) custom-call(bf16[4,64,256]{2,1,0:T(8,128)(2,1)S(1)} %select_convert_fusion.pick, bf16[4,256,64]{2,1,0:T(8,128)(2,1)S(1)} %copy-done.3, bf16[16,2048]{1,0:T(8,128)(2,1)S(1)} %reshape.300.x, bf16[17,4,8,2048]{3,2,1,0:T(8,128)(2,1)} %bitcast.41, ...), custom_call_target="tpu_custom_call" | custom-call | tf_op jit(solution)/shard_map/move_and_project/pallas_call | solution.py:496
  94.4 0.1 add_convert_fusion.1
  94.5 0.1 convert_element_type.47
  94.6 0.1 fusion.11
  94.7 0.1 pad_maximum_fusion
  94.8 0.1 slice_bitcast_fusion
  94.9 0.1 reshape.307
  95.0 0.1 multiply_cosine_fusion.1
  95.1 0.1 subtract_convert_fusion
  95.2 0.1 maximum_bitcast_fusion
  95.3 0.1 reshape.304
  95.4 0.0 copy-start.2
  95.4 2.2 %copy-done.2 = bf16[32,4,8,2048]{3,2,1,0:T(8,128)(2,1)S(1)} copy-done((bf16[32,4,8,2048]{3,2,1,0:T(8,128)(2,1)S(1)}, bf16[32,4,8,2048]{3,2,1,0:T(8,128)(2,1)}, u32[]{:S(2)}) %copy-start.2) | copy-done | bytes 4194328
  97.6 0.0 copy-start.4
  97.6 8.9 %attend.1 = (bf16[64,8,2048]{2,1,0:T(8,128)(2,1)}, bf16[16,16,128]{2,1,0:T(8,128)(2,1)S(1)}) custom-call(s32[64]{0:T(128)S(1)} %compare_select_fusion.2.where_from, s32[2]{0:T(128)S(1)} %dynamic_slice.7.extents, bf16[128,8,2048]{2,1,0:T(8,128)(2,1)S(1)} %bitcast.38, bf16[16,32,128]{2,1,0:T(8,128)(2,1)S(1)} %get-tuple-element.7.q, f32[16,128]{1,0:T(8,128)S(1)} %bitcast.39, ...), custom_call_target="tpu_custom_call" | custom-call | tf_op jit(solution)/shard_map/attend/pallas_call | solution.py:546
  106.5 0.0 copy-done.4
  106.5 29.2 %project_and_sum.1 = bf16[4,8192]{1,0:T(4,128)(2,1)S(1)} custom-call(bf16[4,64,256]{2,1,0:T(8,128)(2,1)S(1)} %copy-done.4, bf16[16,16,128]{2,1,0:T(8,128)(2,1)S(1)} %get-tuple-element.8.mixed, bf16[512,8192]{1,0:T(8,128)(2,1)} %wf_hbm.1), custom_call_target="tpu_custom_call" | custom-call | tf_op jit(solution)/shard_map/project_and_sum/pallas_call | solution.py:575
  135.7 0.7 reshape.305
  (25 shorter events, 0.3 us)
Async XLA Ops:
  0.6 4.1 %copy-start = (s32[64]{0:T(128)S(1)}, s32[64]{0:T(128)}, u32[]{:S(2)}) copy-start(s32[64]{0:T(128)} %param.25) | copy-start | bytes 772
  11.0 4.6 %copy-start.5 = (bf16[8192,64]{0,1:T(8,128)(2,1)S(1)}, bf16[8192,64]{0,1:T(8,128)(2,1)}, u32[]{:S(2)}) copy-start(bf16[8192,64]{0,1:T(8,128)(2,1)} %param.18) | copy-start | bytes 3145732
  16.7 2.8 %copy-start.3 = (bf16[4,256,64]{2,1,0:T(8,128)(2,1)S(1)}, bf16[4,256,64]{2,1,0:T(8,128)(2,1)}, u32[]{:S(2)}) copy-start(bf16[4,256,64]{2,1,0:T(8,128)(2,1)} %constant.92.clone.spread) | copy-start | bytes 393220
  19.4 1.6 %copy-start.1 = (bf16[8192,64]{1,0:T(8,128)(2,1)S(1)}, bf16[8192,64]{1,0:T(8,128)(2,1)}, u32[]{:S(2)}) copy-start(bf16[8192,64]{1,0:T(8,128)(2,1)} %copy.44.wv_hbm) | copy-start | bytes 3145732
  95.4 2.2 %copy-start.2 = (bf16[32,4,8,2048]{3,2,1,0:T(8,128)(2,1)S(1)}, bf16[32,4,8,2048]{3,2,1,0:T(8,128)(2,1)}, u32[]{:S(2)}) copy-start(bf16[32,4,8,2048]{3,2,1,0:T(8,128)(2,1)} %get-tuple-element.6) | copy-start | bytes 12582916
  97.6 8.9 %copy-start.4 = (bf16[4,64,256]{2,1,0:T(8,128)(2,1)S(1)}, bf16[4,64,256]{2,1,0:T(8,128)(2,1)}, u32[]{:S(2)}) copy-start(bf16[4,64,256]{2,1,0:T(8,128)(2,1)} %constant.93.clone.squeeze) | copy-start | bytes 393220

commit v2 on v1

--- a/solution.py
+++ b/solution.py
@@ -159,57 +159,70 @@
 
 
 def move_kernel(
-    n, heads, pick, spread, x, send, wq_hbm, wk_hbm, wv_hbm, pages, qkv,
-    xall, wq, wk, wv, outq, local,
+    n, heads, sent, pick, spread, x, blocks_hbm, wq_hbm, wk_hbm, wv_hbm, pages, qkv,
+    blocks, send, xall, wq, wk, wv, outq, local,
     x_ss, x_rs, o_ss, o_rs, p_ss, p_rs, q_ss, q_rs,
 ):
     me = lax.axis_index("cand")
+    load_blocks = pltpu.make_async_copy(blocks_hbm, blocks, local.at[6])
+    load_blocks.start()
     loads = [
         pltpu.make_async_copy(a, b, local.at[i])
         for i, (a, b) in enumerate(((wq_hbm, wq), (wk_hbm, wk), (wv_hbm, wv)))
     ]
     for load in loads:
         load.start()
-    own_page = pltpu.make_async_copy(send.at[me], pages.at[me], local.at[3])
-    own_extra = pltpu.make_async_copy(send.at[n], pages.at[n + me], local.at[4])
-    own_page.start()
-    own_extra.start()
     xall[me] = x[...]
     greet_all(n, me)
     rows = Gather(n, me, x, xall, 0, x_ss, x_rs)
     extra = Gather(n, me, send.at[n], pages, n, o_ss, o_rs)
     rows.start()
-    extra.start()
+    load_blocks.wait()
+    share = send.shape[1]
+
+    def fill(row):
+        for r in range(share):
+            send[row, r] = blocks[sent[row * share + r]]
 
     def page_copy(k):
         device = lax.rem(me + k, n)
         return remote(send.at[device], pages.at[me], p_ss.at[k], p_rs.at[k], device)
 
-    @pl.loop(1, n)
-    def _(k):
+    fill(n)
+    own_extra = pltpu.make_async_copy(send.at[n], pages.at[n + me], local.at[4])
+    own_extra.start()
+    extra.start()
+
+    @pl.loop(1, n)
+    def _(k):
+        fill(lax.rem(me + k, n))
         page_copy(k).start()
 
+    fill(me)
+    own_page = pltpu.make_async_copy(send.at[me], pages.at[me], local.at[3])
+    own_page.start()
     rows.finish()
     for load in loads:
         load.wait()
     flat = xall[...].reshape(n * ROWS, xall.shape[2])
     depth = xall.shape[2]
     q_sum = jnp.zeros((n * 4, wq.shape[1]), F32)
-    k_sum = jnp.zeros((n * 4, wk.shape[1]), F32)
-    v_sum = jnp.zeros((n * 4, wv.shape[1]), F32)
+    k_sum = jnp.zeros((n * 4, wk.shape[0]), F32)
+    v_sum = jnp.zeros((n * 4, wv.shape[0]), F32)
+    across = (((1,), (1,)), ((), ()))
     for c in range(4):
         xc = jnp.dot(pick[c], flat, preferred_element_type=F32).astype(BF)
         part = pl.ds(c * depth, depth)
         q_sum += jnp.dot(xc, wq[part, :], preferred_element_type=F32)
-        k_sum += jnp.dot(xc, wk[part, :], preferred_element_type=F32)
-        v_sum += jnp.dot(xc, wv[part, :], preferred_element_type=F32)
+        k_sum += lax.dot_general(xc, wk[:, part], across, preferred_element_type=F32)
+        v_sum += lax.dot_general(xc, wv[:, part], across, preferred_element_type=F32)
     q16 = q_sum.astype(BF)
     slab = jnp.zeros((n * ROWS, ATTN_DIM), F32)
     for h in range(heads):
         slab += jnp.dot(
             spread[h], q16[:, h * ATTN_DIM : (h + 1) * ATTN_DIM], preferred_element_type=F32
         )
-    pad = ATTN_DIM - wk.shape[1] - wv.shape[1]
+    pad = ATTN_DIM - wk.shape[0] - wv.shape[0]
     parts = [k_sum, v_sum] + ([jnp.zeros((n * 4, pad), F32)] if pad else [])
     kv16 = jnp.concatenate(parts, axis=1).astype(BF)
     kv_slab = jnp.dot(spread[0], kv16, preferred_element_type=F32)
@@ -249,7 +262,7 @@
 
 def attend_kernel(
     n, heads, where_from, extents, pages, q, cos, sin, k_new, v_new, moved, mixed,
-    held, scores, sems, out_sem,
+    held, sems, out_sem,
 ):
     count = held.shape[0]
 
@@ -445,7 +458,6 @@
     sent = jnp.concatenate(
         [sent[:, :share], jnp.sum(sent[:, share:], axis=0, keepdims=True)], axis=0
     )
-    send = candidate_memory_blocks[sent.reshape(-1)].reshape(n + 1, share, page, page_width)
     arriving = lax.dynamic_slice_in_dim(table, me, 1)[0] // spots
     arrived_rank = jnp.sum(
         jnp.where((arriving[:, None] == arriving[None, :]) & before, 1, 0), axis=1
@@ -499,15 +511,17 @@
             jax.ShapeDtypeStruct((2 * n, share, page, page_width), BF),
             jax.ShapeDtypeStruct((n, 2 * ROWS, ATTN_DIM), BF),
         ),
-        in_specs=[vmem, vmem, vmem] + [any_space] * 4,
+        in_specs=[smem, vmem, vmem, vmem] + [any_space] * 4,
         out_specs=(any_space, any_space),
         scratch_shapes=[
+            pltpu.VMEM(candidate_memory_blocks.shape, BF),
+            pltpu.VMEM((n + 1, share, page, page_width), BF),
             pltpu.VMEM((n, ROWS, embed // pieces), BF),
             pltpu.VMEM(asker_matrix.shape, BF),
-            pltpu.VMEM(address_matrix.shape, BF),
-            pltpu.VMEM(content_matrix.shape, BF),
+            pltpu.VMEM(address_matrix.shape[::-1], BF),
+            pltpu.VMEM(content_matrix.shape[::-1], BF),
             pltpu.VMEM((n, 2 * ROWS, ATTN_DIM), BF),
-            dma((6,)),
+            dma((7,)),
             dma((3, 2 * nz)),
             dma((3, 2 * nz)),
             dma((3, 2 * nz)),
@@ -521,7 +535,16 @@
             collective_id=0, has_side_effects=True, vmem_limit_bytes=48 << 20
         ),
         name="move_and_project",
-    )(pick, spread, x, send, asker_matrix, address_matrix, content_matrix)
+    )(
+        sent.reshape(-1),
+        pick,
+        spread,
+        x,
+        candidate_memory_blocks,
+        asker_matrix,
+        address_matrix.T,
+        content_matrix.T,
+    )
 
     positions = extents[:, None] + jnp.arange(tokens, dtype=jnp.int32)[None, :]
     frequencies = ROPE_BASE ** (
@@ -553,7 +576,6 @@
         out_specs=(any_space, vmem),
         scratch_shapes=[
             pltpu.VMEM((count, page, page_width), BF),
-            pltpu.VMEM((8, 128), F32),
             dma((count,)),
             dma,
         ],

time: 137 us -> 131 us (0.956)
  local copies, waits for them, and re-layouts: 15.7 us -> 9.12 us
    gather x1 -> x0, local copies, waits for them, and re-layouts: 4.54 us -> none  [body(): candidate_memory_blocks[sent.reshape(-1)]]
    unnamed x15 -> x13, local copies, waits for them, and re-layouts: 8.42 us -> 6.39 us
where the time goes in v2:
time: 131 us; the launch traced here: 130 us
  Pallas kernels  112 us (85%)
  local copies, waits for them, and re-layouts  9.12 us (7%)
  other arithmetic  8.33 us (6%)
    pallas_call x1, Pallas kernels, body(): pl.pallas_call(functools.partial(move_kernel, n, heads), out_shape=(jax.S...  73.8 us
    pallas_call x1, Pallas kernels, body(): pl.pallas_call(functools.partial(project_kernel, n, heads, chunks), out_s...  29.2 us
    pallas_call x1, Pallas kernels, body(): pl.pallas_call(functools.partial(attend_kernel, n, heads), out_shape=(jax...  8.93 us
    unnamed x13, local copies, waits for them, and re-layouts  6.39 us

profile of v2, /device:TPU:0, one launch (start us, length us, event | category | flops | bytes accessed | tf_op | source)
XLA Modules:
  0.0 130.2 jit_solution(415012831311090427)
XLA Ops:
  0.6 0.0 copy-start
  0.7 0.9 select_reduce_fusion.5
  1.6 0.7 multiply_add_fusion
  2.2 0.8 select_reduce_fusion.3
  3.0 1.0 fusion
  4.1 0.0 copy-done
  4.1 0.7 gather_fusion.1
  4.8 0.1 dynamic_slice.7.extents
  4.8 0.1 add_convert_fusion.1
  4.9 0.1 convert_element_type.47
  5.0 0.1 multiply_cosine_fusion.1
  5.1 0.1 fusion.10
  5.2 0.1 pad_maximum_fusion
  5.3 0.1 iota_add_fusion
  5.4 0.1 add.120
  5.5 0.8 broadcast_compare_fusion
  6.3 0.7 convert_element_type.44
  7.0 1.0 fusion.2
  8.0 0.1 copy.44
  8.1 0.8 copy.35
  8.9 0.6 gather_fusion
  9.5 0.1 reshape.267
  9.6 0.2 select_reduce_fusion.2
  9.9 0.4 select_reduce_fusion
  10.2 0.3 select_reduce_fusion.1
  10.6 0.1 fusion.11
  10.7 0.1 reshape.268.sent
  10.8 0.7 select_convert_fusion.pick
  11.5 0.0 copy-start.2
  11.5 1.2 copy-done.2
  12.7 0.0 copy-start.3
  12.7 1.2 copy-done.3
  13.9 0.0 copy-start.4
  13.9 0.9 copy-done.4
  14.9 73.8 %move_and_project.1 = (bf16[32,4,8,2048]{3,2,1,0:T(8,128)(2,1)}, bf16[16,32,128]{2,1,0:T(8,128)(2,1)S(1)}) custom-call(s32[68]{0:T(128)S(1)} %reshape.268.sent, bf16[4,64,256]{2,1,0:T(8,128)(2,1)S(1)} %select_convert_fusion.pick, bf16[4,256,64]{2,1,0:T(8,128)(2,1)S(1)} %copy-done.4, bf16[16,2048]{1,0:T(8,128)(2,1)S(1)} %reshape.270.x, ...), custom_call_target="tpu_custom_call" | custom-call | tf_op jit(solution)/shard_map/move_and_project/pallas_call | solution.py:508
  88.7 0.0 copy-start.5
  88.7 0.1 slice_bitcast_fusion
  88.8 0.1 reshape.272
  88.9 0.1 reshape.275
  89.0 0.1 subtract_convert_fusion
  89.1 0.1 maximum_bitcast_fusion
  89.2 0.0 copy-start.1
  89.2 2.2 %copy-done.1 = bf16[32,4,8,2048]{3,2,1,0:T(8,128)(2,1)S(1)} copy-done((bf16[32,4,8,2048]{3,2,1,0:T(8,128)(2,1)S(1)}, bf16[32,4,8,2048]{3,2,1,0:T(8,128)(2,1)}, u32[]{:S(2)}) %copy-start.1) | copy-done | bytes 4194328
  91.4 8.9 %attend.1 = (bf16[64,8,2048]{2,1,0:T(8,128)(2,1)}, bf16[16,16,128]{2,1,0:T(8,128)(2,1)S(1)}) custom-call(s32[64]{0:T(128)S(1)} %compare_select_fusion.1.where_from, s32[2]{0:T(128)S(1)} %dynamic_slice.7.extents, bf16[128,8,2048]{2,1,0:T(8,128)(2,1)S(1)} %bitcast.37, bf16[16,32,128]{2,1,0:T(8,128)(2,1)S(1)} %get-tuple-element.7.q, f32[16,128]{1,0:T(8,128)S(1)} %bitcast.40, ...), custom_call_target="tpu_custom_call" | custom-call | tf_op jit(solution)/shard_map/attend/pallas_call | solution.py:569
  100.3 0.0 copy-done.5
  100.4 29.2 %project_and_sum.1 = bf16[4,8192]{1,0:T(4,128)(2,1)S(1)} custom-call(bf16[4,64,256]{2,1,0:T(8,128)(2,1)S(1)} %copy-done.5, bf16[16,16,128]{2,1,0:T(8,128)(2,1)S(1)} %get-tuple-element.8.mixed, bf16[512,8192]{1,0:T(8,128)(2,1)} %wf_hbm.1), custom_call_target="tpu_custom_call" | custom-call | tf_op jit(solution)/shard_map/project_and_sum/pallas_call | solution.py:597
  129.5 0.7 reshape.273
  (23 shorter events, 0.3 us)
Async XLA Ops:
  0.6 3.4 %copy-start = (s32[64]{0:T(128)S(1)}, s32[64]{0:T(128)}, u32[]{:S(2)}) copy-start(s32[64]{0:T(128)} %param.25) | copy-start | bytes 772
  11.5 1.2 copy-start.2
  12.7 1.2 copy-start.3
  13.9 0.9 copy-start.4
  88.7 11.6 %copy-start.5 = (bf16[4,64,256]{2,1,0:T(8,128)(2,1)S(1)}, bf16[4,64,256]{2,1,0:T(8,128)(2,1)}, u32[]{:S(2)}) copy-start(bf16[4,64,256]{2,1,0:T(8,128)(2,1)} %constant.91.clone.squeeze) | copy-start | bytes 393220
  89.2 2.2 %copy-start.1 = (bf16[32,4,8,2048]{3,2,1,0:T(8,128)(2,1)S(1)}, bf16[32,4,8,2048]{3,2,1,0:T(8,128)(2,1)}, u32[]{:S(2)}) copy-start(bf16[32,4,8,2048]{3,2,1,0:T(8,128)(2,1)} %get-tuple-element.6) | copy-start | bytes 12582916

commit v3 on v2

--- a/solution.py
+++ b/solution.py
@@ -532,7 +532,7 @@
             dma((n,)),
         ],
         compiler_params=pltpu.CompilerParams(
-            collective_id=0, has_side_effects=True, vmem_limit_bytes=48 << 20
+            collective_id=0, has_side_effects=True, vmem_limit_bytes=60 << 20
         ),
         name="move_and_project",
     )(
@@ -579,7 +579,7 @@
             dma((count,)),
             dma,
         ],
-        compiler_params=pltpu.CompilerParams(vmem_limit_bytes=32 << 20),
+        compiler_params=pltpu.CompilerParams(vmem_limit_bytes=60 << 20),
         name="attend",
     )(
         where_from,
@@ -618,7 +618,7 @@
             dma((chunks, nz)),
         ],
         compiler_params=pltpu.CompilerParams(
-            collective_id=1, has_side_effects=True, vmem_limit_bytes=48 << 20
+            collective_id=1, has_side_effects=True, vmem_limit_bytes=60 << 20
         ),
         name="project_and_sum",
     )(squeeze, mixed, final_matrix)

time: 131 us -> 131 us (level)
  other arithmetic: 8.33 us -> 10.4 us
    unnamed x13 -> x5, local copies, waits for them, and re-layouts: 6.39 us -> 0.81 us
    pallas_call x1, Pallas kernels: 8.93 us -> 6.71 us  [body(): pl.pallas_call(functools.partial(attend_kernel, n, heads), out_shape=(jax...]
    pallas_call x1, Pallas kernels: 29.2 us -> 30.7 us  [body(): pl.pallas_call(functools.partial(project_kernel, n, heads, chunks), out_s...]
where the time goes in v3:
time: 131 us
  Pallas kernels  112 us (85%)
  other arithmetic  10.4 us (8%)
  local copies, waits for them, and re-layouts  7.94 us (6%)
    pallas_call x1, Pallas kernels, body(): pl.pallas_call(functools.partial(move_kernel, n, heads), out_shape=(jax.S...  74.2 us
    pallas_call x1, Pallas kernels, body(): pl.pallas_call(functools.partial(project_kernel, n, heads, chunks), out_s...  30.7 us
    pallas_call x1, Pallas kernels, body(): pl.pallas_call(functools.partial(attend_kernel, n, heads), out_shape=(jax...  6.71 us

profile of v3, /device:TPU:0, one launch (start us, length us, event | category | flops | bytes accessed | tf_op | source)
XLA Modules:
  0.0 130.7 jit_solution(3691336651645606783)
XLA Ops:
  0.6 0.0 copy-start
  0.7 0.9 select_reduce_fusion.5
  1.6 0.7 multiply_add_fusion
  2.2 0.8 select_reduce_fusion.3
  3.0 1.0 fusion
  4.1 0.0 copy-done
  4.1 0.7 gather_fusion.1
  4.8 0.1 dynamic_slice.7.extents
  4.8 0.0 copy-start.1
  4.8 0.1 add_convert_fusion.1
  4.9 0.1 convert_element_type.47
  5.0 0.1 multiply_cosine_fusion.1
  5.1 0.1 fusion.10
  5.2 0.1 pad_maximum_fusion
  5.3 0.6 tile.8
  5.9 0.6 tile.20
  6.5 0.1 iota_add_fusion
  6.6 0.1 add.120
  6.7 0.8 broadcast_compare_fusion
  7.5 0.7 convert_element_type.44
  8.2 1.0 fusion.2
  9.2 0.1 copy.44
  9.3 0.6 reshape.270.x
  9.9 0.8 copy.35
  10.7 0.6 gather_fusion
  11.3 0.1 reshape.267
  11.4 0.2 select_reduce_fusion.2
  11.6 0.6 compare_select_fusion.1.where_from
  12.2 0.4 select_reduce_fusion
  12.6 0.3 select_reduce_fusion.1
  12.9 0.1 fusion.11
  13.0 0.6 reshape.268.sent
  13.7 1.4 %select_convert_fusion.pick = bf16[4,64,256]{2,1,0:T(8,128)(2,1)} fusion(pred[4,256]{1,0:T(4,128)(4,1)} %constant.98, pred[64,256]{1,0:T(8,128)(4,1)S(1)} %broadcast_compare_fusion), kind=kLoop, calls=%fused_computation.3 | loop fusion | flops 196608 | bytes 148480 | tf_op jit(solution)/shard_map/convert_element_type | solution.py:487
  15.1 74.2 %move_and_project.1 = (bf16[32,4,8,2048]{3,2,1,0:T(8,128)(2,1)}, bf16[16,32,128]{2,1,0:T(8,128)(2,1)}) custom-call(s32[68]{0:T(128)} %reshape.268.sent, bf16[4,64,256]{2,1,0:T(8,128)(2,1)} %select_convert_fusion.pick, bf16[4,256,64]{2,1,0:T(8,128)(2,1)} %constant.90.clone.spread, bf16[16,2048]{1,0:T(8,128)(2,1)} %reshape.270.x, ...), custom_call_target="tpu_custom_call" | custom-call | tf_op jit(solution)/shard_map/move_and_project/pallas_call | solution.py:508
  89.3 0.0 copy-done.1
  89.3 0.9 slice_bitcast_fusion
  90.2 0.1 reshape.272
  90.3 0.6 pad.8.v_new
  90.9 0.1 reshape.275
  91.0 0.1 subtract_convert_fusion
  91.1 0.1 maximum_bitcast_fusion
  91.2 0.6 pad.7.k_new
  91.8 6.7 %attend.1 = (bf16[64,8,2048]{2,1,0:T(8,128)(2,1)}, bf16[16,16,128]{2,1,0:T(8,128)(2,1)}) custom-call(s32[64]{0:T(128)} %compare_select_fusion.1.where_from, s32[2]{0:T(128)} %copy-done.1, bf16[128,8,2048]{2,1,0:T(8,128)(2,1)} %bitcast.37, bf16[16,32,128]{2,1,0:T(8,128)(2,1)} %get-tuple-element.7.q, f32[16,128]{1,0:T(8,128)} %bitcast.41, f32[16,128]{1,0:T(8,128)} %bitcast.42, ...), custom_call_target="tpu_custom_call" | custom-call | tf_op jit(solution)/shard_map/attend/pallas_call | solution.py:569
  98.5 30.7 %project_and_sum.1 = bf16[4,8192]{1,0:T(4,128)(2,1)} custom-call(bf16[4,64,256]{2,1,0:T(8,128)(2,1)} %constant.91.clone.squeeze, bf16[16,16,128]{2,1,0:T(8,128)(2,1)} %get-tuple-element.8.mixed, bf16[512,8192]{1,0:T(8,128)(2,1)} %wf_hbm.1), custom_call_target="tpu_custom_call" | custom-call | tf_op jit(solution)/shard_map/project_and_sum/pallas_call | solution.py:597
  129.2 1.5 %reshape.273 = bf16[2,2,8192]{2,1,0:T(2,128)(2,1)} reshape(bf16[4,8192]{1,0:T(4,128)(2,1)} %project_and_sum.1) | data formatting | bytes 131072 | tf_op jit(solution)/shard_map/reshape | solution.py:626
  (17 shorter events, 0.2 us)
Async XLA Ops:
  0.6 3.4 %copy-start = (s32[64]{0:T(128)S(1)}, s32[64]{0:T(128)}, u32[]{:S(2)}) copy-start(s32[64]{0:T(128)} %param.25) | copy-start | bytes 772
  4.8 84.5 %copy-start.1 = (s32[2]{0:T(128)}, s32[2]{0:T(128)S(1)}, u32[]{:S(2)}) copy-start(s32[2]{0:T(128)S(1)} %dynamic_slice.7.extents) | copy-start | bytes 28
